TPU v7x, 512 devices: a whole 4x8x8 slice. The times are simulated.
512 devices in a mesh: dp: 16 (over y, core), expert: 32 (over z, x).
Axes of the slice: x: 4, y: 8, z: 8, core: 2. Of those that a mesh axis runs over, the one named last changes fastest.
Arguments:
- stream_q: bfloat16 [4096, 4096], P('dp', 'expert'), may hold values from -6 to 6
- stream_k: bfloat16 [4096, 4096], P('dp', 'expert'), may hold values from -6 to 6
- stream_v: bfloat16 [4096, 4096], P('dp', 'expert'), may hold values from -6 to 6
- conv_taps: float32 [3, 3, 4096], P(None, None, 'expert'), may hold values from -14 to 14
- norm_gain: bfloat16 [4096], P('expert'), may hold values from 0.3984375 to 1.59375
- slot_token: int32 [16, 384], P('dp'), may hold values from 0 to 256, as said below
- expert_count: int32 [16, 2], P('dp'), may hold values from 0 to 256, as said below
- route_prob: float32 [4096], P('dp'), may hold values from 0.25 to 1
- w_proj: bfloat16 [4096, 2, 8192], P('dp', None, 'expert'), may hold values from -0.09375 to 0.09375
- grad_out: bfloat16 [4096, 8192], P('dp', 'expert'), may hold values from -0.75 to 0.75
Outputs:
- activation: bfloat16 [4096, 8192], P('dp', 'expert')
- weight_grad: float32 [4096, 2, 8192], P('dp', None, 'expert')
Inputs may be any that keep to these rules, and one draw needn't show every extreme that they name: `slot_token`: for each index of dp the slots hold its 256 local token numbers, each exactly once, grouped by expert in expert order; each group starts at a multiple of 128 and is padded with the value 256 up to a multiple of 128; all slots after the last group hold 256. `expert_count`: the size of each expert's group in slot_token, before padding; each row sums to 256.
All inputs are finite; a program needn't handle non-finite values.
Results may differ from a plain program's by a relative error of at most 0.023.
Values may be sent and summed in bfloat16 or wider, within the bound.
No kernel may reach another device: no remote copies, remote signals or barrier semaphores. Data moves between devices by JAX's collectives and lax.ppermute only.
A program may use at most 64 MiB of HBM per device.

v0:
```python
import jax
import jax.numpy as jnp
from jax import lax
from jax.sharding import PartitionSpec as P

D = 4096
BLOCK = 128
epsilon = 1e-06


def from_behind(value, axis, steps):
    count = lax.axis_size(axis)
    leading, last = (max(0, -steps), min(count, count - steps))
    return lax.ppermute(value, axis, [(source, source + steps) for source in range(leading, last)])


def block_owner(counts, num_blocks):
    padded = (counts + BLOCK - 1) // BLOCK * BLOCK
    ends = jnp.cumsum(padded)
    starts = jnp.arange(num_blocks, dtype=jnp.int32) * BLOCK
    owner = jnp.sum((starts[:, None] >= ends[None, :]).astype(jnp.int32), axis=1)
    return jnp.minimum(owner, counts.shape[0] - 1)


def on_device(
    stream_q,
    stream_k,
    stream_v,
    conv_taps,
    norm_gain,
    slot_token,
    expert_count,
    route_prob,
    w_proj,
    grad_out,
):
    stacked = jnp.stack([stream_q, stream_k, stream_v])
    before = from_behind(stacked[:, -2:, :], "dp", 1)
    extended = jnp.concatenate([before, stacked], axis=1).astype(jnp.float32)
    convolved = (
        conv_taps[:, 0, None, :] * extended[:, 2:]
        + conv_taps[:, 1, None, :] * extended[:, 1:-1]
        + conv_taps[:, 2, None, :] * extended[:, :-2]
    )
    mixed = (convolved[0] * convolved[1] * convolved[2]).astype(jnp.bfloat16)
    mixed_f = mixed.astype(jnp.float32)
    total = lax.psum(jnp.sum(mixed_f * mixed_f, axis=1), "expert")
    inv_rms = lax.rsqrt(total / D + epsilon)
    normed = (mixed_f * inv_rms[:, None] * norm_gain.astype(jnp.float32)).astype(jnp.bfloat16)
    gathered = lax.all_gather(normed, "expert", axis=1, tiled=True)
    tok_count = gathered.shape[0]
    slots = slot_token[0]
    num_blocks = slots.shape[0] // BLOCK
    owner = block_owner(expert_count[0], num_blocks)
    padded_rows = jnp.concatenate(
        [gathered, jnp.zeros((1, gathered.shape[1]), jnp.bfloat16)], axis=0
    )
    x_blocks = padded_rows[slots].reshape(num_blocks, BLOCK, gathered.shape[1])
    hid_local = w_proj.shape[2]
    experts_here = w_proj.shape[1]
    selector = (owner[:, None] == jnp.arange(experts_here, dtype=jnp.int32)[None, :]).astype(
        jnp.bfloat16
    )
    columns = x_blocks
    chosen_w = jnp.einsum(
        "neh,be->bnh",
        lax.all_gather(w_proj, "dp", axis=0, tiled=True),
        selector,
        preferred_element_type=jnp.float32,
    ).astype(jnp.bfloat16)
    pre_act = jnp.einsum("brn,bnh->brh", columns, chosen_w, preferred_element_type=jnp.float32)
    pre_act = pre_act.reshape(num_blocks * BLOCK, hid_local)
    slot_prob = jnp.concatenate([route_prob, jnp.zeros((1,), jnp.float32)])[slots][:, None]
    sigmoid_z = jax.nn.sigmoid(pre_act)
    hidden = (slot_prob * pre_act * sigmoid_z).astype(jnp.bfloat16)
    activation = (
        jnp.zeros((tok_count + 1, hid_local), jnp.bfloat16).at[slots].set(hidden)[:tok_count]
    )
    slot_grad = jnp.concatenate([grad_out, jnp.zeros((1, hid_local), jnp.bfloat16)], axis=0)[
        slots
    ].astype(jnp.float32)
    grad_pre = (slot_grad * slot_prob * sigmoid_z * (1.0 + pre_act * (1.0 - sigmoid_z))).astype(
        jnp.bfloat16
    )
    grad_blocks = grad_pre.reshape(num_blocks, BLOCK, hid_local)
    masked_grad = grad_blocks[None, :, :, :] * selector.T[:, :, None, None]
    columns = x_blocks
    weight_grad = lax.psum_scatter(
        jnp.einsum(
            "brd,ebrh->deh", columns, masked_grad, preferred_element_type=jnp.float32
        ).astype(jnp.bfloat16),
        "dp",
        scatter_dimension=0,
        tiled=True,
    ).astype(jnp.float32)
    return (activation, weight_grad)


def solution(mesh):
    placed = (
        P("dp", "expert"),
        P("dp", "expert"),
        P("dp", "expert"),
        P(None, None, "expert"),
        P("expert"),
        P("dp", None),
        P("dp", None),
        P("dp"),
        P("dp", None, "expert"),
        P("dp", "expert"),
    )
    return jax.shard_map(
        on_device,
        mesh=mesh,
        in_specs=placed,
        out_specs=(P("dp", "expert"), P("dp", None, "expert")),
        check_vma=False,
    )
```

profile of v0, /device:TPU:29, one launch (start us, length us, event | category | flops | bytes accessed | tf_op | source)
XLA Modules:
  0.0 303.6 jit_solution(1994741817525698117)
XLA Ops:
  7.2 0.7 pad_maximum_fusion.1
  8.0 5.0 %collective-permute-start = (bf16[3,2,128]{2,1,0:T(2,128)(2,1)S(1)}, bf16[3,2,128]{2,1,0:T(2,128)(2,1)S(1)}, u32[]{:S(2)}, u32[]{:S(2)}) collective-permute-start(bf16[3,2,128]{2,1,0:T(2,128)(2,1)S(1)} %pad_maximum_fusion.1), channel_id=1, source_target_pairs={{0,32},{32,64},{64,96},{96,128},{128,160},{160,192},{192,224},{224... | collective-permute-start | bytes 4616 | tf_op jit(solution)/shard_map/ppermute | solution.py:14
  12.9 0.8 fusion.29
  13.8 0.7 convert_element_type.59
  14.4 0.9 maximum_convert_fusion
  15.6 62.6 %psum.7 = f32[256]{0:T(256)S(1)} all-reduce(f32[256]{0:T(256)S(1)} %get-tuple-element.10), channel_id=1, replica_groups=mesh['dp'=16,'expert'=32] {'expert'}, use_global_device_ids=true, to_apply=%region_1.0 | all-reduce | flops 256 | bytes 2048 | tf_op jit(solution)/shard_map/psum | solution.py:47
  78.2 0.7 fusion.17
  79.0 0.7 all-gather.5.cloned.1.call-update
  79.8 0.7 pad_maximum_fusion
  80.5 0.7 fusion.24
  81.2 2.8 gather_fusion
  84.0 2.6 gather_fusion.2
  86.6 0.2 reduce-window.8
  86.9 81.5 %all-gather.3.cloned.1.call-done = bf16[256,4096]{1,0:T(8,128)(2,1)} async-done(((bf16[256,128]{1,0:T(8,128)(2,1)}), bf16[256,4096]{1,0:T(8,128)(2,1)}) %all-gather.3.cloned.1.call-update) | async-done | bytes 2097168 | tf_op jit(solution)/shard_map/all_gather | solution.py:50
  168.4 1.8 concatenate.14
  170.1 4.1 %gather_fusion.1 = bf16[384,4096]{1,0:T(8,128)(2,1)} fusion(bf16[257,4096]{1,0:T(8,128)(2,1)S(1)} %concatenate.14, s32[1024]{0:T(1024)S(1)} %pad_clamp_fusion), kind=kCustom, calls=%fused_computation.1 | custom fusion | bytes 6292992 | tf_op jit(solution)/shard_map/gather | solution.py:58
  174.2 42.7 %all-gather.5.cloned.1.call-done = bf16[4096,2,256]{2,1,0:T(2,128)(2,1)} async-done(((bf16[256,2,256]{2,1,0:T(2,128)(2,1)}), bf16[4096,2,256]{2,1,0:T(2,128)(2,1)}) %all-gather.5.cloned.1.call-update) | async-done | bytes 4194320 | tf_op jit(solution)/shard_map/all_gather | solution.py:67
  217.0 7.5 %convolution_convert_fusion = bf16[3,4096,256]{2,0,1:T(4,128)(2,1)S(1)} fusion(bf16[4096,2,256]{2,1,0:T(2,128)(2,1)} %all-gather.5.cloned.1.call-done, s32[3]{0:T(128)S(1)} %broadcast_minimum_fusion), kind=kOutput, calls=%fused_computation.5 | convolution fusion | flops 15728646 | bytes 10485772 | tf_op jit(solution)/shard_map/neh,be->bnh/dot_general | solution.py:65
  224.5 1.3 fusion.6
  225.8 4.4 %bitcast_convert_fusion = bf16[4096,2,256]{2,0,1:T(8,128)(2,1)} fusion(bf16[3,128,4096,1]{2,1,0,3:T(8,128)(2,1)S(1)} %bitcast.50, bf16[2,3]{1,0:T(2,128)(2,1)S(1)} %compare_convert_fusion, bf16[3,128,256]{2,1,0:T(8,128)(2,1)S(1)} %get-tuple-element.15), kind=kOutput, calls=%fused_computation.4 | convolution fusion | flops 1613496320 | bytes 7536652 | tf_op jit(solution)/shard_map/brd,ebrh->deh/dot_general | solution.py:89
  230.3 1.9 scatter_custom_fusion
  232.2 0.7 slice.56
  232.8 62.2 %reduce-scatter.2.cloned.1.call-done = bf16[256,2,256]{2,0,1:T(8,128)(2,1)} async-done(((bf16[4096,2,256]{2,0,1:T(8,128)(2,1)}), bf16[256,2,256]{2,0,1:T(8,128)(2,1)}) %reduce-scatter.2.cloned.1.call-update) | async-done | bytes 262160 | tf_op jit(solution)/shard_map/reduce_scatter | solution.py:88
  295.1 2.0 copy.21
  (27 shorter events, 0.7 us)
Async XLA Ops:
  7.2 76.8 %copy-start.2 = (bf16[256,256]{1,0:T(8,128)(2,1)S(1)}, bf16[256,256]{1,0:T(8,128)(2,1)}, u32[]{:S(2)}) copy-start(bf16[256,256]{1,0:T(8,128)(2,1)} %param.19) | copy-start | bytes 393220
  7.2 79.4 %copy-start.3 = (s32[1,2]{1,0:T(1,128)S(1)}, s32[1,2]{1,0:T(1,128)}, u32[]{:S(2)}) copy-start(s32[1,2]{1,0:T(1,128)} %param.16) | copy-start | bytes 28
  7.2 161.2 %all-gather.3.cloned.1.call-start = ((), (), s32[]{:S(2)}) async-start(), calls=%async_computation.1 | async-start | bytes 2162688 | tf_op jit(solution)/shard_map/all_gather | solution.py:50
  8.0 6.5 %collective-permute-start = (bf16[3,2,128]{2,1,0:T(2,128)(2,1)S(1)}, bf16[3,2,128]{2,1,0:T(2,128)(2,1)S(1)}, u32[]{:S(2)}, u32[]{:S(2)}) collective-permute-start(bf16[3,2,128]{2,1,0:T(2,128)(2,1)S(1)} %pad_maximum_fusion.1), channel_id=1, source_target_pairs={{0,32},{32,64},{64,96},{96,128},{128,160},{160,192},{192,224},{224... | collective-permute-start | bytes 4616 | tf_op jit(solution)/shard_map/ppermute | solution.py:14
  79.0 138.0 %all-gather.5.cloned.1.call-start = ((), (), s32[]{:S(2)}) async-start(), calls=%async_computation.2 | async-start | bytes 4456448 | tf_op jit(solution)/shard_map/all_gather | solution.py:67
  79.7 215.3 %reduce-scatter.2.cloned.1.call-start = ((), (), s32[]{:S(2)}) async-start(), calls=%async_computation.3 | async-start | bytes 4456448 | tf_op jit(solution)/shard_map/reduce_scatter | solution.py:88
  174.2 50.2 %copy-start = (bf16[384,4096]{1,0:T(8,128)(2,1)S(1)}, bf16[384,4096]{1,0:T(8,128)(2,1)}, u32[]{:S(2)}) copy-start(bf16[384,4096]{1,0:T(8,128)(2,1)} %gather_fusion.1) | copy-start | bytes 9437188
  217.0 7.5 %copy-start.1 = (bf16[384,256]{1,0:T(8,128)(2,1)S(1)}, bf16[384,256]{1,0:T(8,128)(2,1)}, u32[]{:S(2)}) copy-start(bf16[384,256]{1,0:T(8,128)(2,1)} %gather_fusion.2) | copy-start | bytes 589828
Sparse Core Ops, SparseCore 0:
  79.1 89.2 all-gather.2
  170.5 46.4 all-gather.4
  230.3 64.7 reduce-scatter.1
where the time goes:
time: 304 us
  waiting for transfers between devices  187 us (62%)
  blocking collectives  62.6 us (21%)
  local copies, waits for them, and re-layouts  16.6 us (5%)
  between operations  13.9 us (5%)
  matrix products  13.1 us (4%)
  other arithmetic  5.15 us (2%)
  starting transfers between devices  5.08 us (2%)
    all_gather x1, waiting for transfers between devices, on_device(): gathered = lax.all_gather(normed, 'expert', axis=1, tiled=True)  81.5 us
    psum x1, blocking collectives, on_device(): total = lax.psum(jnp.sum(mixed_f * mixed_f, axis=1), 'expert')  62.6 us
    reduce_scatter x1, waiting for transfers between devices, on_device(): lax.psum_scatter(jnp.einsum('brd,ebrh->deh', columns, masked_grad, prefer...  62.2 us
    all_gather x1, waiting for transfers between devices, on_device(): lax.all_gather(w_proj, 'dp', axis=0, tiled=True)  42.7 us
    dot_general x1, matrix products, on_device(): jnp.einsum('neh,be->bnh', lax.all_gather(w_proj, 'dp', axis=0, tiled=True...  7.48 us
  transfers between devices with their start and end apart: 4, of which 3 were waited for; matrix products, arithmetic and copies ran while one was open for 6% of the time, Pallas kernels for 0%

commit v1 on v0

--- a/solution.py
+++ b/solution.py
@@ -6,6 +6,13 @@
 D = 4096
 BLOCK = 128
 epsilon = 1e-06
+
+
+def exchange_gather(block, axis, dim):
+    size = lax.axis_size(axis)
+    tiles = jnp.stack([block for _ in range(size)])
+    tiles = lax.all_to_all(tiles, axis, split_axis=0, concat_axis=0)
+    return jnp.concatenate(tiles, axis=dim)
 
 
 def from_behind(value, axis, steps):
@@ -64,7 +71,7 @@
     columns = x_blocks
     chosen_w = jnp.einsum(
         "neh,be->bnh",
-        lax.all_gather(w_proj, "dp", axis=0, tiled=True),
+        exchange_gather(w_proj, "dp", 0),
         selector,
         preferred_element_type=jnp.float32,
     ).astype(jnp.bfloat16)

time: 304 us -> 362 us (1.19)
  the two profiles are of different devices: /device:TPU:29 before, /device:TPU:25 now
where the time goes in v1:
time: 362 us; the launch traced here: 361 us
  waiting for transfers between devices  231 us (64%)
  blocking collectives  64.5 us (18%)
  local copies, waits for them, and re-layouts  21.5 us (6%)
  starting transfers between devices  15.2 us (4%)
  between operations  14.3 us (4%)
  matrix products  13.3 us (4%)
    ppermute x1, waiting for transfers between devices, from_behind(): lax.ppermute(value, axis, [(source, source + steps) for source in range(l...  85.9 us
    all_gather x1, waiting for transfers between devices, on_device(): gathered = lax.all_gather(normed, 'expert', axis=1, tiled=True)  80.3 us
    reduce_scatter x1, waiting for transfers between devices, on_device(): lax.psum_scatter(jnp.einsum('brd,ebrh->deh', columns, masked_grad, prefer...  65 us
    psum x1, blocking collectives, on_device(): total = lax.psum(jnp.sum(mixed_f * mixed_f, axis=1), 'expert')  64.5 us
    all_to_all x1, starting transfers between devices, exchange_gather(): tiles = lax.all_to_all(tiles, axis, split_axis=0, concat_axis=0)  10.3 us
    dot_general x1, matrix products, on_device(): jnp.einsum('neh,be->bnh', exchange_gather(w_proj, 'dp', 0), selector, pre...  7.6 us
  transfers between devices with their start and end apart: 4, of which 3 were waited for; matrix products, arithmetic and copies ran while one was open for 4% of the time, Pallas kernels for 0%

profile of v1, /device:TPU:25, one launch (start us, length us, event | category | flops | bytes accessed | tf_op | source)
XLA Modules:
  0.0 361.4 jit_solution(1844329088786999391)
XLA Ops:
  7.2 6.2 %stack.14 = bf16[16,256,2,256]{3,2,1,0:T(2,128)(2,1)} broadcast(bf16[256,2,256]{2,1,0:T(2,128)(2,1)} %param.18), dimensions={1,2,3} | broadcast | bytes 4456448 | tf_op jit(solution)/shard_map/stack | solution.py:13
  13.4 10.3 %all-to-all-start = ((bf16[16,256,2,256]{3,2,1,0:T(2,128)(2,1)}), bf16[16,256,2,256]{3,2,1,0:T(2,128)(2,1)}, u32[]{:S(2)}, u32[]{:S(2)}) async-start(bf16[16,256,2,256]{3,2,1,0:T(2,128)(2,1)} %stack.14), calls=%async_computation | async-start | bytes 8388608 | tf_op jit(solution)/shard_map/all_to_all | solution.py:14
  23.8 4.6 %collective-permute-start = (bf16[3,2,128]{2,1,0:T(2,128)(2,1)S(1)}, bf16[3,2,128]{2,1,0:T(2,128)(2,1)S(1)}, u32[]{:S(2)}, u32[]{:S(2)}) collective-permute-start(bf16[3,2,128]{2,1,0:T(2,128)(2,1)S(1)} %pad_maximum_fusion.1), channel_id=1, source_target_pairs={{0,32},{32,64},{64,96},{96,128},{128,160},{160,192},{192,224},{224... | collective-permute-start | bytes 4616 | tf_op jit(solution)/shard_map/ppermute | solution.py:21
  28.5 85.9 %collective-permute-done = bf16[3,2,128]{2,1,0:T(2,128)(2,1)S(1)} collective-permute-done((bf16[3,2,128]{2,1,0:T(2,128)(2,1)S(1)}, bf16[3,2,128]{2,1,0:T(2,128)(2,1)S(1)}, u32[]{:S(2)}, u32[]{:S(2)}) %collective-permute-start) | collective-permute-done | bytes 1568 | tf_op jit(solution)/shard_map/ppermute | solution.py:21
  114.4 0.1 fusion.2
  114.5 0.1 fusion.15
  114.6 64.5 %psum.7 = f32[256]{0:T(256)S(1)} all-reduce(f32[256]{0:T(256)S(1)} %get-tuple-element.8), channel_id=1, replica_groups=mesh['dp'=16,'expert'=32] {'expert'}, use_global_device_ids=true, to_apply=%region_1.0 | all-reduce | flops 256 | bytes 2048 | tf_op jit(solution)/shard_map/psum | solution.py:54
  179.1 0.7 fusion.17
  179.9 0.2 reduce-scatter.2.cloned.1.call-start
  180.2 2.8 gather_fusion
  183.0 2.1 gather_fusion.2
  185.1 0.2 reduce-window.8
  185.3 0.1 fusion.25
  185.4 80.3 %all-gather.2.cloned.1.call-done = bf16[256,4096]{1,0:T(8,128)(2,1)} async-done(((bf16[256,128]{1,0:T(8,128)(2,1)}), bf16[256,4096]{1,0:T(8,128)(2,1)}) %all-gather.2.cloned.1.call-update) | async-done | bytes 2097168 | tf_op jit(solution)/shard_map/all_gather | solution.py:57
  265.7 1.8 concatenate.14
  267.5 4.0 %gather_fusion.1 = bf16[384,4096]{1,0:T(8,128)(2,1)} fusion(bf16[257,4096]{1,0:T(8,128)(2,1)S(1)} %concatenate.14, s32[1024]{0:T(1024)S(1)} %pad_clamp_fusion), kind=kCustom, calls=%fused_computation.1 | custom fusion | bytes 6292992 | tf_op jit(solution)/shard_map/gather | solution.py:65
  271.5 7.6 %convolution_convert_fusion = bf16[3,4096,256]{2,0,1:T(4,128)(2,1)S(1)} fusion(bf16[4096,2,256]{2,1,0:T(2,128)(2,1)} %bitcast.10, s32[3]{0:T(128)S(1)} %broadcast_minimum_fusion), kind=kOutput, calls=%fused_computation.5 | convolution fusion | flops 15728646 | bytes 10485772 | tf_op jit(solution)/shard_map/neh,be->bnh/dot_general | solution.py:72
  279.2 1.3 fusion.6
  280.4 4.4 %bitcast_convert_fusion = bf16[4096,2,256]{2,0,1:T(8,128)(2,1)} fusion(bf16[3,128,4096,1]{2,1,0,3:T(8,128)(2,1)S(1)} %bitcast.51, bf16[2,3]{1,0:T(2,128)(2,1)S(1)} %compare_convert_fusion, bf16[3,128,256]{2,1,0:T(8,128)(2,1)S(1)} %get-tuple-element.13), kind=kOutput, calls=%fused_computation.4 | convolution fusion | flops 1613496320 | bytes 7536652 | tf_op jit(solution)/shard_map/brd,ebrh->deh/dot_general | solution.py:96
  284.9 0.1 fusion.8
  285.0 1.9 scatter_custom_fusion
  286.9 0.7 slice.56
  287.6 65.0 %reduce-scatter.2.cloned.1.call-done = bf16[256,2,256]{2,0,1:T(8,128)(2,1)} async-done(((bf16[4096,2,256]{2,0,1:T(8,128)(2,1)}), bf16[256,2,256]{2,0,1:T(8,128)(2,1)}) %reduce-scatter.2.cloned.1.call-update) | async-done | bytes 262160 | tf_op jit(solution)/shard_map/reduce_scatter | solution.py:95
  352.6 2.0 copy.18
  (39 shorter events, 0.3 us)
Async XLA Ops:
  13.3 10.5 %copy-start.1 = (bf16[256,128]{1,0:T(8,128)(2,1)S(1)}, bf16[256,128]{1,0:T(8,128)(2,1)}, u32[]{:S(2)}) copy-start(bf16[256,128]{1,0:T(8,128)(2,1)} %param.12) | copy-start | bytes 196612
  13.3 10.5 %copy-start.2 = (bf16[256,128]{1,0:T(8,128)(2,1)S(1)}, bf16[256,128]{1,0:T(8,128)(2,1)}, u32[]{:S(2)}) copy-start(bf16[256,128]{1,0:T(8,128)(2,1)} %param.11) | copy-start | bytes 196612
  13.3 10.5 %copy-start.3 = (bf16[256,128]{1,0:T(8,128)(2,1)S(1)}, bf16[256,128]{1,0:T(8,128)(2,1)}, u32[]{:S(2)}) copy-start(bf16[256,128]{1,0:T(8,128)(2,1)} %param.10) | copy-start | bytes 196612
  13.3 15.1 %copy-start.5 = (f32[3,3,128]{2,1,0:T(4,128)S(1)}, f32[3,3,128]{2,1,0:T(4,128)}, u32[]{:S(2)}) copy-start(f32[3,3,128]{2,1,0:T(4,128)} %param.13) | copy-start | bytes 13828
  13.3 15.1 %copy-start.8 = (bf16[128]{0:T(256)(128)(2,1)S(1)}, bf16[128]{0:T(256)(128)(2,1)}, u32[]{:S(2)}) copy-start(bf16[128]{0:T(256)(128)(2,1)} %param.14) | copy-start | bytes 772
  13.3 166.8 %copy-start.7 = (f32[256]{0:T(256)S(1)}, f32[256]{0:T(256)}, u32[]{:S(2)}) copy-start(f32[256]{0:T(256)} %param.17) | copy-start | bytes 3076
  13.4 166.8 %copy-start.6 = (s32[1,384]{1,0:T(1,128)S(1)}, s32[1,384]{1,0:T(1,128)}, u32[]{:S(2)}) copy-start(s32[1,384]{1,0:T(1,128)} %param.15) | copy-start | bytes 4612
  13.4 258.2 %all-to-all-start = ((bf16[16,256,2,256]{3,2,1,0:T(2,128)(2,1)}), bf16[16,256,2,256]{3,2,1,0:T(2,128)(2,1)}, u32[]{:S(2)}, u32[]{:S(2)}) async-start(bf16[16,256,2,256]{3,2,1,0:T(2,128)(2,1)} %stack.14), calls=%async_computation | async-start | bytes 8388608 | tf_op jit(solution)/shard_map/all_to_all | solution.py:14
  23.7 159.3 %copy-start.4 = (bf16[256,256]{1,0:T(8,128)(2,1)S(1)}, bf16[256,256]{1,0:T(8,128)(2,1)}, u32[]{:S(2)}) copy-start(bf16[256,256]{1,0:T(8,128)(2,1)} %param.19) | copy-start | bytes 393220
  23.7 161.3 %copy-start.9 = (s32[1,2]{1,0:T(1,128)S(1)}, s32[1,2]{1,0:T(1,128)}, u32[]{:S(2)}) copy-start(s32[1,2]{1,0:T(1,128)} %param.16) | copy-start | bytes 28
  23.7 242.0 %all-gather.2.cloned.1.call-start = ((), (), s32[]{:S(2)}) async-start(), calls=%async_computation.2 | async-start | bytes 2162688 | tf_op jit(solution)/shard_map/all_gather | solution.py:57
  23.8 90.5 %collective-permute-start = (bf16[3,2,128]{2,1,0:T(2,128)(2,1)S(1)}, bf16[3,2,128]{2,1,0:T(2,128)(2,1)S(1)}, u32[]{:S(2)}, u32[]{:S(2)}) collective-permute-start(bf16[3,2,128]{2,1,0:T(2,128)(2,1)S(1)} %pad_maximum_fusion.1), channel_id=1, source_target_pairs={{0,32},{32,64},{64,96},{96,128},{128,160},{160,192},{192,224},{224... | collective-permute-start | bytes 4616 | tf_op jit(solution)/shard_map/ppermute | solution.py:21
  179.9 172.7 %reduce-scatter.2.cloned.1.call-start = ((), (), s32[]{:S(2)}) async-start(), calls=%async_computation.3 | async-start | bytes 4456448 | tf_op jit(solution)/shard_map/reduce_scatter | solution.py:95
  271.5 7.6 %copy-start = (bf16[384,4096]{1,0:T(8,128)(2,1)S(1)}, bf16[384,4096]{1,0:T(8,128)(2,1)}, u32[]{:S(2)}) copy-start(bf16[384,4096]{1,0:T(8,128)(2,1)} %gather_fusion.1) | copy-start | bytes 9437188
Sparse Core Ops, SparseCore 0:
  180.0 85.6 all-gather.1
  285.0 67.5 reduce-scatter.1
